TPU v7x, 32 devices: a whole 2x2x4 slice. The times are simulated.
32 devices in a mesh: grp: 4 (over z), mem: 8 (over y, x, core).
Axes of the slice: x: 2, y: 2, z: 4, core: 2. Of those that a mesh axis runs over, the one named last changes fastest.
Arguments:
- amplitudes: bfloat16 [8, 2048, 256], P('grp', 'mem'), may hold values from -6 to 6
- integrals: bfloat16 [16, 64, 8192], P('grp', None, 'mem'), may hold values from -0.5 to 0.5
- block_list: int32 [4, 4], replicated, may hold values from 0 to 15, as said below
- block_count: int32 [4], replicated, may hold values from 1 to 4, as said below
- block_slot: int32 [16], replicated, may hold values from 0 to 15, as said below
Outputs:
- residual: float32 [8, 2048, 8192], P('grp', None, 'mem')
Inputs may be any that keep to these rules, and one draw needn't show every extreme that they name: `block_list`: each row holds distinct blocks. Of one row's blocks, at most 2 have slots owned by the same grp index, and some row has exactly 2 such among its live positions. `block_count`: some list is full in every draw. `block_slot`: A permutation of the slots.
All inputs are finite; a program needn't handle non-finite values.
Results may differ from a plain program's by a relative error of at most 0.0003.
Values may be sent and summed in bfloat16 or wider, within the bound.
A program may use at most 128 MiB of HBM per device.

v0:
```python
import jax
import jax.numpy as jnp
from jax import lax
from jax.sharding import PartitionSpec as P

CAP = 2


def per_device(amplitudes, integrals, block_list, block_count, block_slot):
    groups = lax.axis_size("grp")
    own_group = lax.axis_index("grp")
    listed = block_list.shape[1]
    slot_count = integrals.shape[0]
    tile_rows = integrals.shape[1]
    columns = integrals.shape[2]
    slot_table = block_slot[block_list]
    owner_group = slot_table // slot_count
    local_slot = slot_table % slot_count
    positions = jnp.arange(listed, dtype=jnp.int32)
    is_live = positions[None, :] < block_count[:, None]
    earlier_same = (owner_group[:, :, None] == owner_group[:, None, :]) & is_live[:, None, :]
    earlier_same = earlier_same & (positions[None, None, :] < positions[None, :, None])
    order_rank = jnp.sum(earlier_same.astype(jnp.int32), axis=2)
    own_count = lax.dynamic_index_in_dim(block_count, own_group, 0, False)
    own_owner = lax.dynamic_index_in_dim(owner_group, own_group, 0, False)
    own_rank = lax.dynamic_index_in_dim(order_rank, own_group, 0, False)
    own_live = positions < own_count
    wanted = is_live & (owner_group == own_group)
    rank_range = jnp.arange(CAP, dtype=jnp.int32)
    picked = wanted[:, None, :] & (order_rank[:, None, :] == rank_range[None, :, None])
    slot_range = jnp.arange(slot_count, dtype=jnp.int32)
    choose_local = picked[:, :, :, None] & (
        local_slot[:, None, :, None] == slot_range[None, None, None, :]
    )
    choose_local = jnp.sum(choose_local.astype(jnp.int32), axis=2)
    outgoing = jnp.dot(
        choose_local.reshape(groups * CAP, slot_count).astype(jnp.bfloat16),
        integrals.reshape(slot_count, tile_rows * columns),
        preferred_element_type=jnp.float32,
    ).astype(jnp.bfloat16)
    outgoing = outgoing.reshape(groups, CAP, tile_rows, columns)
    incoming = lax.all_to_all(outgoing, "grp", split_axis=0, concat_axis=0, tiled=True)
    target = own_owner * CAP + own_rank
    placing = own_live[:, None] & (
        target[:, None] == jnp.arange(groups * CAP, dtype=jnp.int32)[None, :]
    )
    selected = jnp.dot(
        placing.astype(jnp.bfloat16),
        incoming.reshape(groups * CAP, tile_rows * columns),
        preferred_element_type=jnp.float32,
    ).astype(jnp.bfloat16)
    weights = selected.reshape(listed * tile_rows, columns)
    return jnp.einsum(
        "irk,kc->irc",
        lax.all_gather(amplitudes, "mem", axis=1, tiled=True),
        weights,
        preferred_element_type=jnp.float32,
    )


def solution(mesh):
    in_specs = (P("grp", "mem", None), P("grp", None, "mem"), P(), P(), P())
    out_specs = P("grp", None, "mem")
    return jax.shard_map(
        per_device, mesh=mesh, in_specs=in_specs, out_specs=out_specs, check_vma=False
    )
```

profile of v0, /device:TPU:0, one launch (start us, length us, event | category | flops | bytes accessed | tf_op | source)
XLA Modules:
  0.0 79.8 jit_solution(3979701695162943247)
XLA Ops:
  6.5 0.0 copy-start
  6.5 0.0 copy-start.2
  6.5 0.0 copy-start.1
  6.5 0.0 all-gather.2.cloned.1.call-start
  6.5 0.7 all-gather.2.cloned.1.call-update
  7.3 0.7 compare_select_fusion
  8.0 0.1 reshape.151
  8.0 0.0 copy-done
  8.1 0.7 gather_fusion
  8.7 0.1 reshape.150
  8.8 0.0 copy-done.2
  8.8 0.1 compare_and_fusion.1
  8.9 0.2 convert_reduce_fusion.1
  9.1 0.1 iota_compare_fusion
  9.2 0.1 convert_reduce_fusion
  9.3 0.0 copy-done.1
  9.3 0.4 copy.14
  9.7 0.4 convolution_convert_fusion
  10.2 1.5 %copy.15 = bf16[1,8,64,1024]{3,2,1,0:T(8,128)(2,1)} copy(bf16[1,8,64,1024]{3,1,2,0:T(8,128)(2,1)S(1)} %bitcast.23) | data formatting | bytes 2097152
  11.7 6.3 %all-to-all-start = ((bf16[4,2,64,1024]{3,2,1,0:T(8,128)(2,1)}), bf16[4,2,64,1024]{3,2,1,0:T(8,128)(2,1)S(1)}, u32[]{:S(2)}, u32[]{:S(2)}) async-start(bf16[4,2,64,1024]{3,2,1,0:T(8,128)(2,1)} %bitcast.9), calls=%async_computation | async-start | bytes 2097152 | tf_op jit(solution)/shard_map/all_to_all | solution.py:42
  18.0 0.6 dynamic_slice.11
  18.6 0.6 iota_compare_fusion.4
  19.3 24.5 %all-to-all-done = bf16[4,2,64,1024]{3,2,1,0:T(8,128)(2,1)S(1)} async-done(((bf16[4,2,64,1024]{3,2,1,0:T(8,128)(2,1)}), bf16[4,2,64,1024]{3,2,1,0:T(8,128)(2,1)S(1)}, u32[]{:S(2)}, u32[]{:S(2)}) %all-to-all-start) | async-done | bytes 1048608 | tf_op jit(solution)/shard_map/all_to_all | solution.py:42
  43.8 0.6 copy.16
  44.3 0.5 convolution_convert_fusion.1
  44.8 0.4 reshape.148
  45.3 0.0 all-gather.2.cloned.1.call-done
  45.3 9.7 %convolution_bitcast_fusion = f32[2,2048,1024]{1,2,0:T(8,128)} fusion(bf16[2,2048,256]{2,1,0:T(8,128)(2,1)} %all-gather.2.cloned.1.call-done, bf16[256,1024]{1,0:T(8,128)(2,1)S(1)} %reshape.148), kind=kOutput, calls=%fused_computation.3 | convolution fusion | flops 2147483648 | bytes 19398656 | tf_op jit(solution)/shard_map/irk,kc->irc/dot_general | solution.py:53
  55.0 18.0 %copy.11 = f32[2,2048,1024]{2,1,0:T(8,128)} copy(f32[2,2048,1024]{1,2,0:T(8,128)} %convolution_bitcast_fusion) | data formatting | bytes 33554432 | tf_op jit(solution)/shard_map/irk,kc->irc/dot_general | solution.py:53
  (5 shorter events, 0.0 us)
Async XLA Ops:
  6.5 1.5 %copy-start = (s32[16]{0:T(128)S(1)}, s32[16]{0:T(128)}, u32[]{:S(2)}) copy-start(s32[16]{0:T(128)} %param.9) | copy-start | bytes 196
  6.5 2.3 %copy-start.2 = (s32[4]{0:T(128)S(1)}, s32[4]{0:T(128)}, u32[]{:S(2)}) copy-start(s32[4]{0:T(128)} %param.8) | copy-start | bytes 52
  6.5 2.8 %copy-start.1 = (bf16[4,64,1024]{2,1,0:T(8,128)(2,1)S(1)}, bf16[4,64,1024]{2,1,0:T(8,128)(2,1)}, u32[]{:S(2)}) copy-start(bf16[4,64,1024]{2,1,0:T(8,128)(2,1)} %param.6) | copy-start | bytes 1572868
  6.5 38.7 %all-gather.2.cloned.1.call-start = ((), (), s32[]{:S(2)}) async-start(), calls=%async_computation.1 | async-start | bytes 2359296 | tf_op jit(solution)/shard_map/all_gather | solution.py:55
  11.7 32.0 %all-to-all-start = ((bf16[4,2,64,1024]{3,2,1,0:T(8,128)(2,1)}), bf16[4,2,64,1024]{3,2,1,0:T(8,128)(2,1)S(1)}, u32[]{:S(2)}, u32[]{:S(2)}) async-start(bf16[4,2,64,1024]{3,2,1,0:T(8,128)(2,1)} %bitcast.9), calls=%async_computation | async-start | bytes 2097152 | tf_op jit(solution)/shard_map/all_to_all | solution.py:42
Sparse Core Ops, SparseCore 0:
  9.3 30.5 all-gather.1
where the time goes:
time: 80.3 us; the launch traced here: 79.8 us
  waiting for transfers between devices  25.2 us (31%)
  local copies, waits for them, and re-layouts  22.4 us (28%)
  between operations  13.5 us (17%)
  matrix products  10.6 us (13%)
  starting transfers between devices  6.32 us (8%)
  other arithmetic  1.81 us (2%)
    all_to_all x1, waiting for transfers between devices, per_device(): lax.all_to_all(outgoing, 'grp', split_axis=0, concat_axis=0, tiled=True)  24.5 us
    dot_general x1, local copies, waits for them, and re-layouts, per_device(): jnp.einsum('irk,kc->irc', lax.all_gather(amplitudes, 'mem', axis=1, tiled...  18 us
    dot_general x1, matrix products, per_device(): jnp.einsum('irk,kc->irc', lax.all_gather(amplitudes, 'mem', axis=1, tiled...  9.74 us
    all_to_all x1, starting transfers between devices, per_device(): lax.all_to_all(outgoing, 'grp', split_axis=0, concat_axis=0, tiled=True)  6.32 us
    unnamed x9, local copies, waits for them, and re-layouts  2.55 us
  transfers between devices with their start and end apart: 2, of which 1 were waited for; matrix products, arithmetic and copies ran while one was open for 9% of the time, Pallas kernels for 0%

commit v1 on v0

v1 whole, which is shorter than its diff:
```python
import functools

import jax
import jax.numpy as jnp
from jax import lax
from jax.experimental import pallas as pl
from jax.experimental.pallas import tpu as pltpu
from jax.sharding import PartitionSpec as P

CAP = 2
MESH = pl.DeviceIdType.MESH
CHUNKS = 2


def exchange_kernel(
    groups, tiles_ref, list_ref, count_ref, slot_ref, amp_ref, all_ref, recv_ref,
    stage, own_sem, z_send, z_recv, a_send, a_recv,
):
    z = lax.axis_index("grp")
    m = lax.axis_index("mem")
    c, x, y = m % 2, (m // 2) % 2, m // 4
    sib = (y * 2 + x) * 2 + (1 - c)
    xn = (y * 2 + (1 - x)) * 2 + c
    yn = ((1 - y) * 2 + x) * 2 + c
    dg = ((1 - y) * 2 + (1 - x)) * 2 + c
    slots = tiles_ref.shape[0]
    listed = list_ref.shape[1]
    occ, rows = amp_ref.shape[0], amp_ref.shape[1]
    part = rows // CHUNKS
    pieces = [(i, h) for h in range(CHUNKS) for i in range(occ)]

    barrier = pltpu.get_barrier_semaphore()
    near = [(z, sib), (z, xn), (z, yn)]
    far = [(lax.rem(z + d, groups), m) for d in range(1, groups)]
    for device in near + far:
        pl.semaphore_signal(barrier, inc=1, device_id=device, device_id_type=MESH)

    def block(owner, piece):
        i, h = piece
        return all_ref.at[i, pl.ds(pl.multiple_of(owner * rows + h * part, 16), part)]

    own = pltpu.make_async_copy(
        amp_ref, all_ref.at[:, pl.ds(pl.multiple_of(m * rows, 16), rows)], own_sem
    )
    own.start()

    for d in range(1, groups):
        r = lax.rem(z + d, groups)
        seen = jnp.int32(0)
        first = jnp.int32(0)
        second = jnp.int32(0)
        for l in range(listed):
            slot = slot_ref[list_ref[r, l]]
            hit = (slot // slots == z) & (l < count_ref[r])
            local = slot % slots
            first = jnp.where(hit & (seen == 0), local, first)
            second = jnp.where(hit & (seen == 1), local, second)
            seen = seen + hit.astype(jnp.int32)
        stage[(d - 1) * CAP] = tiles_ref[first]
        stage[(d - 1) * CAP + 1] = tiles_ref[second]
    pl.semaphore_wait(barrier, len(near) + len(far))

    copies = []
    for d in (2, 3, 1) if groups == 4 else range(1, groups):
        r = lax.rem(z + d, groups)
        for k in range(CAP):
            index = (d - 1) * CAP + k
            copy = pltpu.make_async_remote_copy(
                stage.at[index], recv_ref.at[z * CAP + k],
                z_send.at[index], z_recv.at[index],
                device_id=(r, m), device_id_type=MESH,
            )
            copies.append(copy)

    def send(kind, k, source, owner, target):
        copy = pltpu.make_async_remote_copy(
            source, block(owner, pieces[k]),
            a_send.at[kind, k], a_recv.at[kind, k],
            device_id=(z, target), device_id_type=MESH,
        )
        copy.start()
        copies.append(copy)
        return copy

    count = len(pieces)
    from_x, from_y, from_dg = [], [], []
    mine = [amp_ref.at[i, pl.ds(h * part, part)] for i, h in pieces]
    for k in range(count):
        from_x.append(send(0, k, mine[k], m, xn))
        from_y.append(send(1, k, mine[k], m, yn))
        if k == 0:
            for copy in copies[: (groups - 1) * CAP]:
                copy.start()
    for k in range(count):
        send(2, k, mine[k], m, sib)
    arrived = []
    for k in range(count):
        from_x[k].wait_recv()
        if k % 2 == 0:
            from_dg.append(send(3, k, block(xn, pieces[k]), xn, yn))
        send(4, k, block(xn, pieces[k]), xn, sib)
        from_y[k].wait_recv()
        if k % 2 == 1:
            from_dg.append(send(3, k, block(yn, pieces[k]), yn, xn))
        send(5, k, block(yn, pieces[k]), yn, sib)
    for k in range(count):
        from_dg[k].wait_recv()
        send(6, k, block(dg, pieces[k]), dg, sib)
    waited = {id(copy) for copy in from_x + from_y + from_dg}
    own.wait()
    for copy in copies:
        if id(copy) not in waited:
            copy.wait_recv()
    for copy in copies:
        copy.wait_send()


def exchange(amplitudes, integrals, block_list, block_count, block_slot):
    groups, members = lax.axis_size("grp"), lax.axis_size("mem")
    occ, rows, depth = amplitudes.shape
    tile_rows, columns = integrals.shape[1:]
    count = occ * CHUNKS
    smem = pl.BlockSpec(memory_space=pltpu.SMEM)
    return pl.pallas_call(
        functools.partial(exchange_kernel, groups),
        name="exchange",
        out_shape=(
            jax.ShapeDtypeStruct((occ, rows * members, depth), amplitudes.dtype),
            jax.ShapeDtypeStruct((groups * CAP, tile_rows, columns), integrals.dtype),
        ),
        in_specs=[pl.BlockSpec(memory_space=pltpu.VMEM), smem, smem, smem,
                  pl.BlockSpec(memory_space=pl.ANY)],
        out_specs=(pl.BlockSpec(memory_space=pl.ANY), pl.BlockSpec(memory_space=pl.ANY)),
        scratch_shapes=[
            pltpu.VMEM(((groups - 1) * CAP, tile_rows, columns), integrals.dtype),
            pltpu.SemaphoreType.DMA,
            pltpu.SemaphoreType.DMA(((groups - 1) * CAP,)),
            pltpu.SemaphoreType.DMA(((groups - 1) * CAP,)),
            pltpu.SemaphoreType.DMA((7, count)),
            pltpu.SemaphoreType.DMA((7, count)),
        ],
        compiler_params=pltpu.CompilerParams(
            collective_id=0, has_side_effects=True, vmem_limit_bytes=32 * 2**20
        ),
    )(integrals, block_list, block_count, block_slot, amplitudes)


def product_kernel(
    own_ref, list_ref, count_ref, slot_ref, amp_ref, tiles_ref, recv_ref, out_ref,
    weights, sems,
):
    slots, tile_rows = tiles_ref.shape[0], tiles_ref.shape[1]
    listed = list_ref.shape[1]
    z = own_ref[0]

    @pl.when((pl.program_id(0) == 0) & (pl.program_id(1) == 0))
    def _():
        slot = [slot_ref[list_ref[z, l]] for l in range(listed)]
        live = [l < count_ref[z] for l in range(listed)]
        for l in range(listed):
            owner = slot[l] // slots
            rank = jnp.int32(0)
            for e in range(l):
                rank = rank + (slot[e] // slots == owner).astype(jnp.int32)
            part = weights.at[pl.ds(l * tile_rows, tile_rows)]

            @pl.when(live[l] & (owner == z))
            def _():
                pltpu.make_async_copy(
                    tiles_ref.at[slot[l] % slots], part, sems.at[l]
                ).start()

            @pl.when(live[l] & (owner != z))
            def _():
                pltpu.make_async_copy(
                    recv_ref.at[owner * CAP + rank], part, sems.at[l]
                ).start()

            @pl.when(jnp.logical_not(live[l]))
            def _():
                part[...] = jnp.zeros(part.shape, part.dtype)

        for l in range(listed):
            part = weights.at[pl.ds(l * tile_rows, tile_rows)]

            @pl.when(live[l])
            def _():
                pltpu.make_async_copy(tiles_ref.at[0], part, sems.at[l]).wait()

    out_ref[0] = jnp.dot(
        amp_ref[0], weights[...], preferred_element_type=jnp.float32
    )


def product(amplitudes, integrals, received, block_list, block_count, block_slot):
    occ, rows, depth = amplitudes.shape
    tile_rows, columns = integrals.shape[1:]
    listed = block_list.shape[1]
    step = 256
    own = lax.axis_index("grp").astype(jnp.int32).reshape(1)
    hbm = pl.BlockSpec(memory_space=pl.ANY)
    return pl.pallas_call(
        product_kernel,
        name="product",
        out_shape=jax.ShapeDtypeStruct((occ, rows, columns), jnp.float32),
        grid_spec=pltpu.PrefetchScalarGridSpec(
            num_scalar_prefetch=4,
            grid=(occ, rows // step),
            in_specs=[pl.BlockSpec((1, step, depth), lambda i, r, *_: (i, r, 0)), hbm, hbm],
            out_specs=pl.BlockSpec((1, step, columns), lambda i, r, *_: (i, r, 0)),
            scratch_shapes=[
                pltpu.VMEM((listed * tile_rows, columns), integrals.dtype),
                pltpu.SemaphoreType.DMA((listed,)),
            ],
        ),
        compiler_params=pltpu.CompilerParams(vmem_limit_bytes=32 * 2**20),
    )(own, block_list, block_count, block_slot, amplitudes, integrals, received)


def gathered_path(amplitudes, integrals, block_list, block_count, block_slot):
    groups = lax.axis_size("grp")
    me = lax.axis_index("grp")
    listed = block_list.shape[1]
    slots, tile_rows, columns = integrals.shape
    table = block_slot[block_list]
    owner, local = table // slots, table % slots
    positions = jnp.arange(listed, dtype=jnp.int32)
    same = owner[:, :, None] == owner[:, None, :]
    same = same & (positions[None, None, :] < positions[None, :, None])
    rank = jnp.sum(same.astype(jnp.int32), axis=2)
    live = positions[None, :] < block_count[:, None]
    pick = (live & (owner == me))[:, None, :] & (
        rank[:, None, :] == jnp.arange(CAP, dtype=jnp.int32)[None, :, None]
    )
    sent = jnp.sum(jnp.where(pick, local[:, None, :], 0), axis=2)
    outgoing = integrals[sent.reshape(-1)].reshape(groups, CAP, tile_rows, columns)
    incoming = lax.all_to_all(outgoing, "grp", split_axis=0, concat_axis=0, tiled=True)
    incoming = incoming.reshape(groups * CAP, tile_rows, columns)
    return lax.all_gather(amplitudes, "mem", axis=1, tiled=True), incoming


def per_device(by_kernel, amplitudes, integrals, block_list, block_count, block_slot):
    move = exchange if by_kernel else gathered_path
    rows, received = move(amplitudes, integrals, block_list, block_count, block_slot)
    return product(rows, integrals, received, block_list, block_count, block_slot)


def solution(mesh):
    in_specs = (P("grp", "mem", None), P("grp", None, "mem"), P(), P(), P())
    out_specs = P("grp", None, "mem")
    by_kernel = mesh.shape["mem"] == 8 and mesh.shape["grp"] == 4
    return jax.shard_map(
        functools.partial(per_device, by_kernel), mesh=mesh,
        in_specs=in_specs, out_specs=out_specs, check_vma=False,
    )
```

time: 80.3 us -> 43.2 us (0.54)
  the two profiles are of different devices: /device:TPU:0 before, /device:TPU:16 now
where the time goes in v1:
time: 43.2 us; the launch traced here: 42.7 us
  Pallas kernels  38.7 us (90%)
  local copies, waits for them, and re-layouts  3.98 us (9%)
    pallas_call x1, Pallas kernels, exchange(): pl.pallas_call(functools.partial(exchange_kernel, groups), name='exchange...  27.2 us
    pallas_call x1, Pallas kernels, product(): pl.pallas_call(product_kernel, name='product', out_shape=jax.ShapeDtypeSt...  11.5 us
    unnamed x10, local copies, waits for them, and re-layouts  3.98 us

profile of v1, /device:TPU:16, one launch (start us, length us, event | category | flops | bytes accessed | tf_op | source)
XLA Modules:
  0.0 42.7 jit_solution(11528279377086589848)
XLA Ops:
  0.0 0.0 copy-start
  0.0 1.0 %copy-done = bf16[4,64,1024]{2,1,0:T(8,128)(2,1)S(1)} copy-done((bf16[4,64,1024]{2,1,0:T(8,128)(2,1)S(1)}, bf16[4,64,1024]{2,1,0:T(8,128)(2,1)}, u32[]{:S(2)}) %copy-start) | copy-done | bytes 524312
  1.0 0.0 copy-start.1
  1.0 0.9 %copy-done.1 = bf16[2,256,256]{2,1,0:T(8,128)(2,1)S(1)} copy-done((bf16[2,256,256]{2,1,0:T(8,128)(2,1)S(1)}, bf16[2,256,256]{2,1,0:T(8,128)(2,1)}, u32[]{:S(2)}) %copy-start.1) | copy-done | bytes 262168
  2.0 0.0 copy-start.2
  2.0 0.7 %copy-done.2 = s32[4,4]{1,0:T(4,128)S(1)} copy-done((s32[4,4]{1,0:T(4,128)S(1)}, s32[4,4]{1,0:T(4,128)}, u32[]{:S(2)}) %copy-start.2) | copy-done | bytes 88
  2.7 0.0 copy-start.3
  2.7 0.7 %copy-done.3 = s32[4]{0:T(128)S(1)} copy-done((s32[4]{0:T(128)S(1)}, s32[4]{0:T(128)}, u32[]{:S(2)}) %copy-start.3) | copy-done | bytes 40
  3.3 0.0 copy-start.4
  3.3 0.7 %copy-done.4 = s32[16]{0:T(128)S(1)} copy-done((s32[16]{0:T(128)S(1)}, s32[16]{0:T(128)}, u32[]{:S(2)}) %copy-start.4) | copy-done | bytes 88
  4.0 27.2 %exchange.1 = (bf16[2,2048,256]{2,1,0:T(8,128)(2,1)S(1)}, bf16[8,64,1024]{2,1,0:T(8,128)(2,1)S(1)}) custom-call(bf16[4,64,1024]{2,1,0:T(8,128)(2,1)S(1)} %copy-done, s32[4,4]{1,0:T(4,128)S(1)} %copy-done.2, s32[4]{0:T(128)S(1)} %copy-done.3, s32[16]{0:T(128)S(1)} %copy-done.4, bf16[2,256,256]{2,1,0:T(8,128)(2,1)S(1)} %copy-done.1), custom_call_target="tpu_custom_call" | custom-call | tf_op jit(solution)/shard_map/exchange/pallas_call | solution.py:124
  31.2 11.5 %product.1 = f32[2,2048,1024]{2,1,0:T(8,128)} custom-call(s32[1]{0:T(128)} %bitcast.own_ref, s32[4,4]{1,0:T(4,128)S(1)} %copy-done.2, s32[4]{0:T(128)S(1)} %copy-done.3, s32[16]{0:T(128)S(1)} %copy-done.4, bf16[2,2048,256]{2,1,0:T(8,128)(2,1)S(1)} %get-tuple-element.7.amp_ref, bf16[4,64,1024]{2,1,0:T(8,128)(2,1)S(1)} %copy-done, ...), custom_call_target="tpu_custom_call" | custom-call | tf_op jit(solution)/shard_map/product/pallas_call | solution.py:202
Async XLA Ops:
  0.0 1.0 %copy-start = (bf16[4,64,1024]{2,1,0:T(8,128)(2,1)S(1)}, bf16[4,64,1024]{2,1,0:T(8,128)(2,1)}, u32[]{:S(2)}) copy-start(bf16[4,64,1024]{2,1,0:T(8,128)(2,1)} %tiles_ref.3) | copy-start | bytes 1572868
  1.0 0.9 %copy-start.1 = (bf16[2,256,256]{2,1,0:T(8,128)(2,1)S(1)}, bf16[2,256,256]{2,1,0:T(8,128)(2,1)}, u32[]{:S(2)}) copy-start(bf16[2,256,256]{2,1,0:T(8,128)(2,1)} %amp_ref.1) | copy-start | bytes 786436
  2.0 0.7 %copy-start.2 = (s32[4,4]{1,0:T(4,128)S(1)}, s32[4,4]{1,0:T(4,128)}, u32[]{:S(2)}) copy-start(s32[4,4]{1,0:T(4,128)} %list_ref.3) | copy-start | bytes 196
  2.7 0.7 %copy-start.3 = (s32[4]{0:T(128)S(1)}, s32[4]{0:T(128)}, u32[]{:S(2)}) copy-start(s32[4]{0:T(128)} %count_ref.3) | copy-start | bytes 52
  3.3 0.7 %copy-start.4 = (s32[16]{0:T(128)S(1)}, s32[16]{0:T(128)}, u32[]{:S(2)}) copy-start(s32[16]{0:T(128)} %slot_ref.3) | copy-start | bytes 196

commit v2 on v1

--- a/solution.py
+++ b/solution.py
@@ -12,9 +12,24 @@
 CHUNKS = 2
 
 
+def load_tables(sources, targets, sem):
+    copies = [
+        pltpu.make_async_copy(source, target, sem.at[k])
+        for k, (source, target) in enumerate(zip(sources, targets))
+    ]
+    for copy in copies:
+        copy.start()
+    return copies
+
+
+def table_scratch(block_list, block_count, block_slot):
+    tables = (block_list, block_count, block_slot)
+    return [pltpu.SMEM(t.shape, t.dtype) for t in tables] + [pltpu.SemaphoreType.DMA((3,))]
+
+
 def exchange_kernel(
-    groups, tiles_ref, list_ref, count_ref, slot_ref, amp_ref, all_ref, recv_ref,
-    stage, own_sem, z_send, z_recv, a_send, a_recv,
+    groups, tiles_ref, list_hbm, count_hbm, slot_hbm, amp_ref, all_ref, recv_ref,
+    list_ref, count_ref, slot_ref, table_sem, stage, own_sem, z_send, z_recv, a_send, a_recv,
 ):
     z = lax.axis_index("grp")
     m = lax.axis_index("mem")
@@ -29,6 +44,9 @@
     part = rows // CHUNKS
     pieces = [(i, h) for h in range(CHUNKS) for i in range(occ)]
 
+    tables = load_tables(
+        (list_hbm, count_hbm, slot_hbm), (list_ref, count_ref, slot_ref), table_sem
+    )
     barrier = pltpu.get_barrier_semaphore()
     near = [(z, sib), (z, xn), (z, yn)]
     far = [(lax.rem(z + d, groups), m) for d in range(1, groups)]
@@ -43,6 +61,8 @@
         amp_ref, all_ref.at[:, pl.ds(pl.multiple_of(m * rows, 16), rows)], own_sem
     )
     own.start()
+    for copy in tables:
+        copy.wait()
 
     for d in range(1, groups):
         r = lax.rem(z + d, groups)
@@ -120,7 +140,7 @@
     occ, rows, depth = amplitudes.shape
     tile_rows, columns = integrals.shape[1:]
     count = occ * CHUNKS
-    smem = pl.BlockSpec(memory_space=pltpu.SMEM)
+    hbm = pl.BlockSpec(memory_space=pl.ANY)
     return pl.pallas_call(
         functools.partial(exchange_kernel, groups),
         name="exchange",
@@ -128,10 +148,9 @@
             jax.ShapeDtypeStruct((occ, rows * members, depth), amplitudes.dtype),
             jax.ShapeDtypeStruct((groups * CAP, tile_rows, columns), integrals.dtype),
         ),
-        in_specs=[pl.BlockSpec(memory_space=pltpu.VMEM), smem, smem, smem,
-                  pl.BlockSpec(memory_space=pl.ANY)],
-        out_specs=(pl.BlockSpec(memory_space=pl.ANY), pl.BlockSpec(memory_space=pl.ANY)),
-        scratch_shapes=[
+        in_specs=[pl.BlockSpec(memory_space=pltpu.VMEM)] + [hbm] * 4,
+        out_specs=(hbm, hbm),
+        scratch_shapes=table_scratch(block_list, block_count, block_slot) + [
             pltpu.VMEM(((groups - 1) * CAP, tile_rows, columns), integrals.dtype),
             pltpu.SemaphoreType.DMA,
             pltpu.SemaphoreType.DMA(((groups - 1) * CAP,)),
@@ -146,75 +165,120 @@
 
 
 def product_kernel(
-    own_ref, list_ref, count_ref, slot_ref, amp_ref, tiles_ref, recv_ref, out_ref,
-    weights, sems,
+    step, list_hbm, count_hbm, slot_hbm, amp_hbm, tiles_ref, recv_ref, out_ref,
+    list_ref, count_ref, slot_ref, table_sem, amp, weights, made, sems, amp_sem, out_sem,
 ):
+    occ, rows, depth = amp_hbm.shape
     slots, tile_rows = tiles_ref.shape[0], tiles_ref.shape[1]
     listed = list_ref.shape[1]
-    z = own_ref[0]
-
-    @pl.when((pl.program_id(0) == 0) & (pl.program_id(1) == 0))
-    def _():
-        slot = [slot_ref[list_ref[z, l]] for l in range(listed)]
-        live = [l < count_ref[z] for l in range(listed)]
-        for l in range(listed):
-            owner = slot[l] // slots
-            rank = jnp.int32(0)
-            for e in range(l):
-                rank = rank + (slot[e] // slots == owner).astype(jnp.int32)
-            part = weights.at[pl.ds(l * tile_rows, tile_rows)]
-
-            @pl.when(live[l] & (owner == z))
-            def _():
-                pltpu.make_async_copy(
-                    tiles_ref.at[slot[l] % slots], part, sems.at[l]
-                ).start()
-
-            @pl.when(live[l] & (owner != z))
-            def _():
-                pltpu.make_async_copy(
-                    recv_ref.at[owner * CAP + rank], part, sems.at[l]
-                ).start()
-
-            @pl.when(jnp.logical_not(live[l]))
-            def _():
-                part[...] = jnp.zeros(part.shape, part.dtype)
-
-        for l in range(listed):
-            part = weights.at[pl.ds(l * tile_rows, tile_rows)]
-
-            @pl.when(live[l])
-            def _():
-                pltpu.make_async_copy(tiles_ref.at[0], part, sems.at[l]).wait()
-
-    out_ref[0] = jnp.dot(
-        amp_ref[0], weights[...], preferred_element_type=jnp.float32
-    )
+    z = lax.axis_index("grp")
+    buffers = made.shape[0]
+    per = rows // step
+    tables = load_tables(
+        (list_hbm, count_hbm, slot_hbm), (list_ref, count_ref, slot_ref), table_sem
+    )
+    held = amp.shape[0]
+
+    def fetch(t):
+        return pltpu.make_async_copy(
+            amp_hbm.at[t // per, pl.ds(pl.multiple_of((t % per) * step, 16), step)],
+            amp.at[t % held], amp_sem.at[t % held],
+        )
+
+    for t in range(held):
+        fetch(t).start()
+    for copy in tables:
+        copy.wait()
+
+    def pick(l):
+        return weights.at[pl.ds(pl.multiple_of(l * tile_rows, 16), tile_rows)]
+
+    @pl.loop(0, listed)
+    def _(l):
+        slot = slot_ref[list_ref[z, l]]
+        owner = slot // slots
+        live = l < count_ref[z]
+
+        def count_same(e, rank):
+            return rank + (slot_ref[list_ref[z, e]] // slots == owner).astype(jnp.int32)
+
+        rank = lax.fori_loop(0, l, count_same, jnp.int32(0))
+
+        @pl.when(live & (owner == z))
+        def _():
+            pltpu.make_async_copy(tiles_ref.at[slot % slots], pick(l), sems.at[l]).start()
+
+        @pl.when(live & (owner != z))
+        def _():
+            pltpu.make_async_copy(
+                recv_ref.at[owner * CAP + rank], pick(l), sems.at[l]
+            ).start()
+
+        @pl.when(jnp.logical_not(live))
+        def _():
+            part = pick(l)
+            part[...] = jnp.zeros(part.shape, part.dtype)
+
+    @pl.loop(0, listed)
+    def _(l):
+        @pl.when(l < count_ref[z])
+        def _():
+            pltpu.make_async_copy(tiles_ref.at[0], pick(l), sems.at[l]).wait()
+
+    def put(t):
+        return pltpu.make_async_copy(
+            made.at[t % buffers],
+            out_ref.at[t // per, pl.ds(pl.multiple_of((t % per) * step, 8), step)],
+            out_sem.at[t % buffers],
+        )
+
+    total = occ * per
+
+    @pl.loop(0, total)
+    def _(t):
+        fetch(t).wait()
+
+        @pl.when(t >= buffers)
+        def _():
+            put(t - buffers).wait()
+
+        made[t % buffers] = jnp.dot(
+            amp[t % held], weights[...], preferred_element_type=jnp.float32
+        )
+        put(t).start()
+
+        @pl.when(t + held < total)
+        def _():
+            fetch(t + held).start()
+
+    @pl.loop(total - buffers, total)
+    def _(t):
+        put(t).wait()
 
 
 def product(amplitudes, integrals, received, block_list, block_count, block_slot):
     occ, rows, depth = amplitudes.shape
     tile_rows, columns = integrals.shape[1:]
     listed = block_list.shape[1]
-    step = 256
-    own = lax.axis_index("grp").astype(jnp.int32).reshape(1)
+    step = 128
+    buffers = min(8, occ * rows // step)
     hbm = pl.BlockSpec(memory_space=pl.ANY)
     return pl.pallas_call(
-        product_kernel,
+        functools.partial(product_kernel, step),
         name="product",
         out_shape=jax.ShapeDtypeStruct((occ, rows, columns), jnp.float32),
-        grid_spec=pltpu.PrefetchScalarGridSpec(
-            num_scalar_prefetch=4,
-            grid=(occ, rows // step),
-            in_specs=[pl.BlockSpec((1, step, depth), lambda i, r, *_: (i, r, 0)), hbm, hbm],
-            out_specs=pl.BlockSpec((1, step, columns), lambda i, r, *_: (i, r, 0)),
-            scratch_shapes=[
-                pltpu.VMEM((listed * tile_rows, columns), integrals.dtype),
-                pltpu.SemaphoreType.DMA((listed,)),
-            ],
-        ),
-        compiler_params=pltpu.CompilerParams(vmem_limit_bytes=32 * 2**20),
-    )(own, block_list, block_count, block_slot, amplitudes, integrals, received)
+        in_specs=[hbm] * 6,
+        out_specs=hbm,
+        scratch_shapes=table_scratch(block_list, block_count, block_slot) + [
+            pltpu.VMEM((buffers, step, depth), amplitudes.dtype),
+            pltpu.VMEM((listed * tile_rows, columns), integrals.dtype),
+            pltpu.VMEM((buffers, step, columns), jnp.float32),
+            pltpu.SemaphoreType.DMA((listed,)),
+            pltpu.SemaphoreType.DMA((buffers,)),
+            pltpu.SemaphoreType.DMA((buffers,)),
+        ],
+        compiler_params=pltpu.CompilerParams(vmem_limit_bytes=40 * 2**20),
+    )(block_list, block_count, block_slot, amplitudes, integrals, received)
 
 
 def gathered_path(amplitudes, integrals, block_list, block_count, block_slot):

time: 43.2 us -> 46.7 us (1.081)
  local copies, waits for them, and re-layouts: 3.98 us -> 7.01 us
    unnamed x10 -> x18, local copies, waits for them, and re-layouts: 3.98 us -> 7.01 us
    pallas_call x1, Pallas kernels: 11.5 us -> 12.2 us  [product(): pl.pallas_call(functools.partial(product_kernel, step), name='product', o...]
    pallas_call x1, Pallas kernels: 27.2 us -> 26.6 us  [exchange(): pl.pallas_call(functools.partial(exchange_kernel, groups), name='exchange...]
where the time goes in v2:
time: 46.7 us; the launch traced here: 45.9 us
  Pallas kernels  38.8 us (83%)
  local copies, waits for them, and re-layouts  7.01 us (15%)
    pallas_call x1, Pallas kernels, exchange(): pl.pallas_call(functools.partial(exchange_kernel, groups), name='exchange...  26.6 us
    pallas_call x1, Pallas kernels, product(): pl.pallas_call(functools.partial(product_kernel, step), name='product', o...  12.2 us
    unnamed x18, local copies, waits for them, and re-layouts  7.01 us

profile of v2, /device:TPU:16, one launch (start us, length us, event | category | flops | bytes accessed | tf_op | source)
XLA Modules:
  0.0 45.9 jit_solution(14889278498456747240)
XLA Ops:
  0.0 0.0 copy-start
  0.0 1.0 %copy-done = bf16[4,64,1024]{2,1,0:T(8,128)(2,1)S(1)} copy-done((bf16[4,64,1024]{2,1,0:T(8,128)(2,1)S(1)}, bf16[4,64,1024]{2,1,0:T(8,128)(2,1)}, u32[]{:S(2)}) %copy-start) | copy-done | bytes 524312
  1.0 0.0 copy-start.2
  1.0 0.9 %copy-done.2 = bf16[2,256,256]{2,1,0:T(8,128)(2,1)S(1)} copy-done((bf16[2,256,256]{2,1,0:T(8,128)(2,1)S(1)}, bf16[2,256,256]{2,1,0:T(8,128)(2,1)}, u32[]{:S(2)}) %copy-start.2) | copy-done | bytes 262168
  2.0 0.0 copy-start.3
  2.0 0.7 %copy-done.3 = s32[4,4]{1,0:T(4,128)S(1)} copy-done((s32[4,4]{1,0:T(4,128)S(1)}, s32[4,4]{1,0:T(4,128)}, u32[]{:S(2)}) %copy-start.3) | copy-done | bytes 88
  2.7 0.0 copy-start.5
  2.7 0.7 %copy-done.5 = s32[4]{0:T(128)S(1)} copy-done((s32[4]{0:T(128)S(1)}, s32[4]{0:T(128)}, u32[]{:S(2)}) %copy-start.5) | copy-done | bytes 40
  3.3 0.0 copy-start.7
  3.3 0.7 %copy-done.7 = s32[16]{0:T(128)S(1)} copy-done((s32[16]{0:T(128)S(1)}, s32[16]{0:T(128)}, u32[]{:S(2)}) %copy-start.7) | copy-done | bytes 88
  4.0 26.6 %exchange.1 = (bf16[2,2048,256]{2,1,0:T(8,128)(2,1)S(1)}, bf16[8,64,1024]{2,1,0:T(8,128)(2,1)S(1)}) custom-call(bf16[4,64,1024]{2,1,0:T(8,128)(2,1)S(1)} %copy-done, s32[4,4]{1,0:T(4,128)S(1)} %copy-done.3, s32[4]{0:T(128)S(1)} %copy-done.5, s32[16]{0:T(128)S(1)} %copy-done.7, bf16[2,256,256]{2,1,0:T(8,128)(2,1)S(1)} %copy-done.2), custom_call_target="tpu_custom_call" | custom-call | tf_op jit(solution)/shard_map/exchange/pallas_call | solution.py:144
  30.6 0.0 copy-start.1
  30.6 1.0 %copy-done.1 = bf16[4,64,1024]{2,1,0:T(8,128)(2,1)S(1)} copy-done((bf16[4,64,1024]{2,1,0:T(8,128)(2,1)S(1)}, bf16[4,64,1024]{2,1,0:T(8,128)(2,1)}, u32[]{:S(2)}) %copy-start.1) | copy-done | bytes 524312
  31.7 0.0 copy-start.4
  31.7 0.7 %copy-done.4 = s32[4,4]{1,0:T(4,128)S(1)} copy-done((s32[4,4]{1,0:T(4,128)S(1)}, s32[4,4]{1,0:T(4,128)}, u32[]{:S(2)}) %copy-start.4) | copy-done | bytes 88
  32.4 0.0 copy-start.6
  32.4 0.7 %copy-done.6 = s32[4]{0:T(128)S(1)} copy-done((s32[4]{0:T(128)S(1)}, s32[4]{0:T(128)}, u32[]{:S(2)}) %copy-start.6) | copy-done | bytes 40
  33.0 0.0 copy-start.8
  33.0 0.7 %copy-done.8 = s32[16]{0:T(128)S(1)} copy-done((s32[16]{0:T(128)S(1)}, s32[16]{0:T(128)}, u32[]{:S(2)}) %copy-start.8) | copy-done | bytes 88
  33.7 12.2 %product.1 = f32[2,2048,1024]{2,1,0:T(8,128)} custom-call(s32[4,4]{1,0:T(4,128)S(1)} %copy-done.4, s32[4]{0:T(128)S(1)} %copy-done.6, s32[16]{0:T(128)S(1)} %copy-done.8, bf16[2,2048,256]{2,1,0:T(8,128)(2,1)S(1)} %get-tuple-element.7.amp_hbm, bf16[4,64,1024]{2,1,0:T(8,128)(2,1)S(1)} %copy-done.1, bf16[8,64,1024]{2,1,0:T(8,128)(2,1)S(1)} %get-tuple-element.8.recv_ref), custom_call_target="tpu_custom_call" | custom-call | tf_op jit(solution)/shard_map/product/pallas_call | solution.py:266
Async XLA Ops:
  0.0 1.0 %copy-start = (bf16[4,64,1024]{2,1,0:T(8,128)(2,1)S(1)}, bf16[4,64,1024]{2,1,0:T(8,128)(2,1)}, u32[]{:S(2)}) copy-start(bf16[4,64,1024]{2,1,0:T(8,128)(2,1)} %tiles_ref.3) | copy-start | bytes 1572868
  1.0 0.9 %copy-start.2 = (bf16[2,256,256]{2,1,0:T(8,128)(2,1)S(1)}, bf16[2,256,256]{2,1,0:T(8,128)(2,1)}, u32[]{:S(2)}) copy-start(bf16[2,256,256]{2,1,0:T(8,128)(2,1)} %amp_ref.1) | copy-start | bytes 786436
  2.0 0.7 %copy-start.3 = (s32[4,4]{1,0:T(4,128)S(1)}, s32[4,4]{1,0:T(4,128)}, u32[]{:S(2)}) copy-start(s32[4,4]{1,0:T(4,128)} %list_hbm.3) | copy-start | bytes 196
  2.7 0.7 %copy-start.5 = (s32[4]{0:T(128)S(1)}, s32[4]{0:T(128)}, u32[]{:S(2)}) copy-start(s32[4]{0:T(128)} %count_hbm.3) | copy-start | bytes 52
  3.3 0.7 %copy-start.7 = (s32[16]{0:T(128)S(1)}, s32[16]{0:T(128)}, u32[]{:S(2)}) copy-start(s32[16]{0:T(128)} %slot_hbm.3) | copy-start | bytes 196
  30.6 1.0 %copy-start.1 = (bf16[4,64,1024]{2,1,0:T(8,128)(2,1)S(1)}, bf16[4,64,1024]{2,1,0:T(8,128)(2,1)}, u32[]{:S(2)}) copy-start(bf16[4,64,1024]{2,1,0:T(8,128)(2,1)} %tiles_ref.3) | copy-start | bytes 1572868
  31.7 0.7 %copy-start.4 = (s32[4,4]{1,0:T(4,128)S(1)}, s32[4,4]{1,0:T(4,128)}, u32[]{:S(2)}) copy-start(s32[4,4]{1,0:T(4,128)} %list_hbm.3) | copy-start | bytes 196
  32.4 0.7 %copy-start.6 = (s32[4]{0:T(128)S(1)}, s32[4]{0:T(128)}, u32[]{:S(2)}) copy-start(s32[4]{0:T(128)} %count_hbm.3) | copy-start | bytes 52
  33.0 0.7 %copy-start.8 = (s32[16]{0:T(128)S(1)}, s32[16]{0:T(128)}, u32[]{:S(2)}) copy-start(s32[16]{0:T(128)} %slot_hbm.3) | copy-start | bytes 196

commit v3 on v2

--- a/solution.py
+++ b/solution.py
@@ -140,7 +140,7 @@
     occ, rows, depth = amplitudes.shape
     tile_rows, columns = integrals.shape[1:]
     count = occ * CHUNKS
-    hbm = pl.BlockSpec(memory_space=pl.ANY)
+    hbm = pl.BlockSpec(memory_space=pltpu.HBM)
     return pl.pallas_call(
         functools.partial(exchange_kernel, groups),
         name="exchange",
@@ -181,7 +181,7 @@
 
     def fetch(t):
         return pltpu.make_async_copy(
-            amp_hbm.at[t // per, pl.ds(pl.multiple_of((t % per) * step, 16), step)],
+            amp_hbm.at[t // per, pl.ds((t % per) * step, step)],
             amp.at[t % held], amp_sem.at[t % held],
         )
 
@@ -228,31 +228,22 @@
     def put(t):
         return pltpu.make_async_copy(
             made.at[t % buffers],
-            out_ref.at[t // per, pl.ds(pl.multiple_of((t % per) * step, 8), step)],
+            out_ref.at[t // per, pl.ds((t % per) * step, step)],
             out_sem.at[t % buffers],
         )
 
     total = occ * per
-
-    @pl.loop(0, total)
-    def _(t):
+    for t in range(total):
         fetch(t).wait()
-
-        @pl.when(t >= buffers)
-        def _():
+        if t >= buffers:
             put(t - buffers).wait()
-
         made[t % buffers] = jnp.dot(
             amp[t % held], weights[...], preferred_element_type=jnp.float32
         )
         put(t).start()
-
-        @pl.when(t + held < total)
-        def _():
+        if t + held < total:
             fetch(t + held).start()
-
-    @pl.loop(total - buffers, total)
-    def _(t):
+    for t in range(total - buffers, total):
         put(t).wait()
 
 
@@ -260,9 +251,9 @@
     occ, rows, depth = amplitudes.shape
     tile_rows, columns = integrals.shape[1:]
     listed = block_list.shape[1]
-    step = 128
+    step = 256
     buffers = min(8, occ * rows // step)
-    hbm = pl.BlockSpec(memory_space=pl.ANY)
+    hbm = pl.BlockSpec(memory_space=pltpu.HBM)
     return pl.pallas_call(
         functools.partial(product_kernel, step),
         name="product",

time: 46.7 us -> 43.8 us (0.938)
  Pallas kernels: 38.8 us -> 36.3 us
    pallas_call x1, Pallas kernels: 12.2 us -> 9.7 us  [product(): pl.pallas_call(functools.partial(product_kernel, step), name='product', o...]
where the time goes in v3:
time: 43.8 us; the launch traced here: 43.4 us
  Pallas kernels  36.3 us (83%)
  local copies, waits for them, and re-layouts  7.01 us (16%)
    pallas_call x1, Pallas kernels, exchange(): pl.pallas_call(functools.partial(exchange_kernel, groups), name='exchange...  26.6 us
    pallas_call x1, Pallas kernels, product(): pl.pallas_call(functools.partial(product_kernel, step), name='product', o...  9.7 us
    unnamed x18, local copies, waits for them, and re-layouts  7.01 us

profile of v3, /device:TPU:16, one launch (start us, length us, event | category | flops | bytes accessed | tf_op | source)
XLA Modules:
  0.0 43.4 jit_solution(5531172834508973980)
XLA Ops:
  0.0 0.0 copy-start
  0.0 1.0 %copy-done = bf16[4,64,1024]{2,1,0:T(8,128)(2,1)S(1)} copy-done((bf16[4,64,1024]{2,1,0:T(8,128)(2,1)S(1)}, bf16[4,64,1024]{2,1,0:T(8,128)(2,1)}, u32[]{:S(2)}) %copy-start) | copy-done | bytes 524312
  1.0 0.0 copy-start.2
  1.0 0.9 %copy-done.2 = bf16[2,256,256]{2,1,0:T(8,128)(2,1)S(1)} copy-done((bf16[2,256,256]{2,1,0:T(8,128)(2,1)S(1)}, bf16[2,256,256]{2,1,0:T(8,128)(2,1)}, u32[]{:S(2)}) %copy-start.2) | copy-done | bytes 262168
  2.0 0.0 copy-start.3
  2.0 0.7 %copy-done.3 = s32[4,4]{1,0:T(4,128)S(1)} copy-done((s32[4,4]{1,0:T(4,128)S(1)}, s32[4,4]{1,0:T(4,128)}, u32[]{:S(2)}) %copy-start.3) | copy-done | bytes 88
  2.7 0.0 copy-start.5
  2.7 0.7 %copy-done.5 = s32[4]{0:T(128)S(1)} copy-done((s32[4]{0:T(128)S(1)}, s32[4]{0:T(128)}, u32[]{:S(2)}) %copy-start.5) | copy-done | bytes 40
  3.3 0.0 copy-start.7
  3.3 0.7 %copy-done.7 = s32[16]{0:T(128)S(1)} copy-done((s32[16]{0:T(128)S(1)}, s32[16]{0:T(128)}, u32[]{:S(2)}) %copy-start.7) | copy-done | bytes 88
  4.0 26.6 %exchange.1 = (bf16[2,2048,256]{2,1,0:T(8,128)(2,1)S(1)}, bf16[8,64,1024]{2,1,0:T(8,128)(2,1)S(1)}) custom-call(bf16[4,64,1024]{2,1,0:T(8,128)(2,1)S(1)} %copy-done, s32[4,4]{1,0:T(4,128)S(1)} %copy-done.3, s32[4]{0:T(128)S(1)} %copy-done.5, s32[16]{0:T(128)S(1)} %copy-done.7, bf16[2,256,256]{2,1,0:T(8,128)(2,1)S(1)} %copy-done.2), custom_call_target="tpu_custom_call" | custom-call | tf_op jit(solution)/shard_map/exchange/pallas_call | solution.py:144
  30.6 0.0 copy-start.1
  30.6 1.0 %copy-done.1 = bf16[4,64,1024]{2,1,0:T(8,128)(2,1)S(1)} copy-done((bf16[4,64,1024]{2,1,0:T(8,128)(2,1)S(1)}, bf16[4,64,1024]{2,1,0:T(8,128)(2,1)}, u32[]{:S(2)}) %copy-start.1) | copy-done | bytes 524312
  31.7 0.0 copy-start.4
  31.7 0.7 %copy-done.4 = s32[4,4]{1,0:T(4,128)S(1)} copy-done((s32[4,4]{1,0:T(4,128)S(1)}, s32[4,4]{1,0:T(4,128)}, u32[]{:S(2)}) %copy-start.4) | copy-done | bytes 88
  32.4 0.0 copy-start.6
  32.4 0.7 %copy-done.6 = s32[4]{0:T(128)S(1)} copy-done((s32[4]{0:T(128)S(1)}, s32[4]{0:T(128)}, u32[]{:S(2)}) %copy-start.6) | copy-done | bytes 40
  33.0 0.0 copy-start.8
  33.0 0.7 %copy-done.8 = s32[16]{0:T(128)S(1)} copy-done((s32[16]{0:T(128)S(1)}, s32[16]{0:T(128)}, u32[]{:S(2)}) %copy-start.8) | copy-done | bytes 88
  33.7 9.7 %product.1 = f32[2,2048,1024]{2,1,0:T(8,128)} custom-call(s32[4,4]{1,0:T(4,128)S(1)} %copy-done.4, s32[4]{0:T(128)S(1)} %copy-done.6, s32[16]{0:T(128)S(1)} %copy-done.8, bf16[2,2048,256]{2,1,0:T(8,128)(2,1)S(1)} %get-tuple-element.7.amp_hbm, bf16[4,64,1024]{2,1,0:T(8,128)(2,1)S(1)} %copy-done.1, bf16[8,64,1024]{2,1,0:T(8,128)(2,1)S(1)} %get-tuple-element.8.recv_ref), custom_call_target="tpu_custom_call" | custom-call | tf_op jit(solution)/shard_map/product/pallas_call | solution.py:257
Async XLA Ops:
  0.0 1.0 %copy-start = (bf16[4,64,1024]{2,1,0:T(8,128)(2,1)S(1)}, bf16[4,64,1024]{2,1,0:T(8,128)(2,1)}, u32[]{:S(2)}) copy-start(bf16[4,64,1024]{2,1,0:T(8,128)(2,1)} %tiles_ref.3) | copy-start | bytes 1572868
  1.0 0.9 %copy-start.2 = (bf16[2,256,256]{2,1,0:T(8,128)(2,1)S(1)}, bf16[2,256,256]{2,1,0:T(8,128)(2,1)}, u32[]{:S(2)}) copy-start(bf16[2,256,256]{2,1,0:T(8,128)(2,1)} %amp_ref.1) | copy-start | bytes 786436
  2.0 0.7 %copy-start.3 = (s32[4,4]{1,0:T(4,128)S(1)}, s32[4,4]{1,0:T(4,128)}, u32[]{:S(2)}) copy-start(s32[4,4]{1,0:T(4,128)} %list_hbm.3) | copy-start | bytes 196
  2.7 0.7 %copy-start.5 = (s32[4]{0:T(128)S(1)}, s32[4]{0:T(128)}, u32[]{:S(2)}) copy-start(s32[4]{0:T(128)} %count_hbm.3) | copy-start | bytes 52
  3.3 0.7 %copy-start.7 = (s32[16]{0:T(128)S(1)}, s32[16]{0:T(128)}, u32[]{:S(2)}) copy-start(s32[16]{0:T(128)} %slot_hbm.3) | copy-start | bytes 196
  30.6 1.0 %copy-start.1 = (bf16[4,64,1024]{2,1,0:T(8,128)(2,1)S(1)}, bf16[4,64,1024]{2,1,0:T(8,128)(2,1)}, u32[]{:S(2)}) copy-start(bf16[4,64,1024]{2,1,0:T(8,128)(2,1)} %tiles_ref.3) | copy-start | bytes 1572868
  31.7 0.7 %copy-start.4 = (s32[4,4]{1,0:T(4,128)S(1)}, s32[4,4]{1,0:T(4,128)}, u32[]{:S(2)}) copy-start(s32[4,4]{1,0:T(4,128)} %list_hbm.3) | copy-start | bytes 196
  32.4 0.7 %copy-start.6 = (s32[4]{0:T(128)S(1)}, s32[4]{0:T(128)}, u32[]{:S(2)}) copy-start(s32[4]{0:T(128)} %count_hbm.3) | copy-start | bytes 52
  33.0 0.7 %copy-start.8 = (s32[16]{0:T(128)S(1)}, s32[16]{0:T(128)}, u32[]{:S(2)}) copy-start(s32[16]{0:T(128)} %slot_hbm.3) | copy-start | bytes 196
